TPU v7x, 512 devices: a whole 4x8x8 slice. The times are simulated.
512 devices in a mesh: dp: 128 (over z, y, core), vocab: 4 (over x).
Axes of the slice: x: 4, y: 8, z: 8, core: 2. Of those that a mesh axis runs over, the one named last changes fastest.
Arguments:
- hidden: bfloat16 [16384, 18432], P('dp', 'vocab'), may hold values from -24 to 24
- embed_cot: bfloat16 [16384, 18432], P('dp', 'vocab'), may hold values from -24 to 24
- head_block: bfloat16 [128, 18432], P('vocab'), may hold values from -0.125 to 0.125
- lse_rest: float32 [16384], P('dp'), may hold values from 6 to 12
- token_ids: int32 [16384], P('dp'), may hold values from 0 to 255
- target_ids: int32 [16384], P('dp'), may hold values from 0 to 255
Outputs:
- head_grad: bfloat16 [128, 18432], P('vocab')
Inputs may be any that keep to these rules, and one draw needn't show every extreme that they name: `token_ids`: ids below 128 are rows of the block, the others lie outside it. `target_ids`: ids below 128 are rows of the block, the others lie outside it.
All inputs are finite; a program needn't handle non-finite values.
Results may differ from a plain program's by a relative error of at most 0.0035.
Values may be sent and summed in bfloat16 or wider, within the bound.
A program may use at most 64 MiB of HBM per device.

v0:
```python
import math

import jax
import jax.numpy as jnp
from jax import lax
from jax.sharding import PartitionSpec as P


def replica_sum(gradient):
    shares = lax.psum_scatter(gradient, "dp", scatter_dimension=1, tiled=True).astype(jnp.bfloat16)
    return lax.all_gather(shares, "dp", axis=1, tiled=True)


def gradient_terms(
    exponent, denominator, vocab_rows, token_ids, target_ids, features, cotangents, loss_scale
):
    targets = (target_ids[:, None] == vocab_rows[None, :]).astype(jnp.float32)
    coefficients = (exponent / denominator[:, None] - targets).astype(jnp.bfloat16)
    picks = (token_ids[:, None] == vocab_rows[None, :]).astype(jnp.bfloat16)
    gradient = jnp.dot(coefficients.T, features, preferred_element_type=jnp.float32)
    gradient = gradient + jnp.dot(picks.T, cotangents, preferred_element_type=jnp.float32)
    return gradient * loss_scale


def local(hidden, embed_cot, head_block, lse_rest, token_ids, target_ids):
    n_vocab = lax.axis_size("vocab")
    n_replicas = lax.axis_size("dp")
    tok_rows = hidden.shape[0]
    vocab_dev = head_block.shape[0]
    block_rows = vocab_dev * n_vocab
    loss_scale = math.sqrt(block_rows / (tok_rows * n_replicas))
    features, cotangents = (
        lax.all_gather(hidden, "vocab", axis=1, tiled=True),
        lax.all_gather(embed_cot, "vocab", axis=1, tiled=True),
    )
    logits = jnp.dot(features, head_block.T, preferred_element_type=jnp.float32)
    exponent = jnp.exp(logits)
    block_sum = lax.psum(jnp.sum(exponent, axis=1), "vocab")
    denominator = jnp.exp(lse_rest) + block_sum
    row_start = lax.axis_index("vocab") * vocab_dev
    vocab_rows = row_start + jnp.arange(vocab_dev, dtype=jnp.int32)
    gradient = gradient_terms(
        exponent, denominator, vocab_rows, token_ids, target_ids, features, cotangents, loss_scale
    )
    return replica_sum(gradient)


def solution(mesh):
    return jax.shard_map(
        local,
        mesh=mesh,
        in_specs=(P("dp", "vocab"), P("dp", "vocab"), P("vocab", None), P("dp"), P("dp"), P("dp")),
        out_specs=P("vocab", None),
        check_vma=False,
    )
```

profile of v0, /device:TPU:1, one launch (start us, length us, event | category | flops | bytes accessed | tf_op | source)
XLA Modules:
  0.0 451.7 jit_solution(16787038879448922731)
XLA Ops:
  6.5 0.0 copy-start
  6.5 0.0 all-gather.5.cloned.1.call-start
  6.5 0.7 all-gather.5.cloned.1.call-update
  7.3 0.0 all-gather.7.cloned.1.call-start
  7.3 0.7 all-gather.7.cloned.1.call-update
  8.0 0.0 reduce-scatter.4.cloned.1.call-start
  8.1 0.5 iota_add_fusion
  8.6 64.3 %all-gather.5.cloned.1.call-done = bf16[128,18432]{1,0:T(8,128)(2,1)} async-done(((bf16[128,4608]{1,0:T(8,128)(2,1)}), bf16[128,18432]{1,0:T(8,128)(2,1)}) %all-gather.5.cloned.1.call-update) | async-done | bytes 4718608 | tf_op jit(solution)/shard_map/all_gather | solution.py:33
  72.9 0.0 copy-done
  72.9 4.0 fusion.8
  76.9 6.7 %psum.7 = f32[128]{0:T(128)S(1)} all-reduce(f32[128]{0:T(128)S(1)} %get-tuple-element.5), channel_id=1, replica_groups=mesh['dp'=128,'vocab'=4] {'vocab'}, use_global_device_ids=true, to_apply=%region_1.0 | all-reduce | flops 128 | bytes 1024 | tf_op jit(solution)/shard_map/psum | solution.py:38
  83.6 0.0 copy-done.1
  83.6 3.2 fusion.2
  86.8 46.6 %all-gather.7.cloned.1.call-done = bf16[128,18432]{1,0:T(8,128)(2,1)} async-done(((bf16[128,4608]{1,0:T(8,128)(2,1)}), bf16[128,18432]{1,0:T(8,128)(2,1)}) %all-gather.7.cloned.1.call-update) | async-done | bytes 4718608 | tf_op jit(solution)/shard_map/all_gather | solution.py:34
  133.4 4.6 %fusion = f32[32,18432]{1,0:T(8,128)} fusion(f32[32,18432]{1,0:T(8,128)S(1)} %fusion.2, bf16[128,18432]{1,0:T(8,128)(2,1)} %all-gather.7.cloned.1.call-done, s32[128]{0:T(128)} %param.10, s32[32]{0:T(128)} %iota_add_fusion), kind=kOutput, calls=%fused_computation.1 | convolution fusion | flops 152178688 | bytes 9437824 | tf_op jit(solution)/shard_map/dot_general | solution.py:21
  138.0 6.8 %copy.9 = f32[32,18432]{0,1:T(8,128)} copy(f32[32,18432]{1,0:T(8,128)} %fusion) | data formatting | bytes 4718592
  144.8 0.0 reduce-scatter.4.cloned.1.call-update
  144.8 0.0 all-gather.9.cloned.1.call-start
  144.8 204.8 %reduce-scatter.4.cloned.1.call-done = f32[144,32]{1,0:T(8,128)} async-done(((f32[18432,32]{1,0:T(8,128)}), f32[144,32]{1,0:T(8,128)}) %reduce-scatter.4.cloned.1.call-update) | async-done | bytes 18448
  349.7 1.6 copy.10
  351.2 0.0 all-gather.9.cloned.1.call-update
  351.3 87.0 %all-gather.9.cloned.1.call-done = bf16[128,144,32]{1,2,0:T(8,128)(2,1)} async-done(((bf16[1,144,32]{1,2,0:T(8,128)(2,1)}), bf16[128,144,32]{1,2,0:T(8,128)(2,1)}) %all-gather.9.cloned.1.call-update) | async-done | bytes 1179664 | tf_op jit(solution)/shard_map/all_gather | solution.py:11
  438.2 2.8 copy.8
  441.0 4.2 reshape.8
  (2 shorter events, 0.0 us)
Async XLA Ops:
  6.5 66.4 %copy-start = (bf16[32,18432]{1,0:T(8,128)(2,1)S(1)}, bf16[32,18432]{1,0:T(8,128)(2,1)}, u32[]{:S(2)}) copy-start(bf16[32,18432]{1,0:T(8,128)(2,1)} %param.8) | copy-start | bytes 3538948
  6.5 66.3 %all-gather.5.cloned.1.call-start = ((), (), s32[]{:S(2)}) async-start(), calls=%async_computation.1 | async-start | bytes 5898240 | tf_op jit(solution)/shard_map/all_gather | solution.py:33
  7.3 126.2 %all-gather.7.cloned.1.call-start = ((), (), s32[]{:S(2)}) async-start(), calls=%async_computation.2 | async-start | bytes 5898240 | tf_op jit(solution)/shard_map/all_gather | solution.py:34
  8.0 341.7 %reduce-scatter.4.cloned.1.call-start = ((), (), s32[]{:S(2)}) async-start(), calls=%async_computation.4 | async-start | bytes 9510912
  8.6 75.1 %copy-start.1 = (f32[128]{0:T(128)S(1)}, f32[128]{0:T(128)}, u32[]{:S(2)}) copy-start(f32[128]{0:T(128)} %param.9) | copy-start | bytes 1540
  144.8 293.5 %all-gather.9.cloned.1.call-start = ((), (), s32[]{:S(2)}) async-start(), calls=%async_computation.3 | async-start | bytes 2113536 | tf_op jit(solution)/shard_map/all_gather | solution.py:11
Sparse Core Ops, SparseCore 0:
  9.5 63.3 all-gather.4
  75.0 58.4 all-gather.6
  144.9 204.7 reduce-scatter.3
  353.1 85.0 all-gather.8
where the time goes:
time: 452 us
  waiting for transfers between devices  404 us (89%)
  local copies, waits for them, and re-layouts  15.3 us (3%)
  between operations  13.1 us (3%)
  matrix products  11.8 us (3%)
  blocking collectives  6.68 us (1%)
    unnamed x5, waiting for transfers between devices  206 us
    all_gather x1, waiting for transfers between devices, replica_sum(): return lax.all_gather(shares, 'dp', axis=1, tiled=True)  87 us
    all_gather x1, waiting for transfers between devices, local(): lax.all_gather(hidden, 'vocab', axis=1, tiled=True)  64.3 us
    all_gather x1, waiting for transfers between devices, local(): lax.all_gather(embed_cot, 'vocab', axis=1, tiled=True)  46.6 us
    unnamed x7, local copies, waits for them, and re-layouts  12.5 us
  transfers between devices with their start and end apart: 4, of which 4 were waited for; matrix products, arithmetic and copies ran while one was open for 2% of the time, Pallas kernels for 0%

commit v1 on v0

v1 whole, which is shorter than its diff:
```python
import functools
import math

import jax
import jax.numpy as jnp
from jax import lax
from jax.experimental import pallas as pl
from jax.experimental.pallas import tpu as pltpu
from jax.sharding import PartitionSpec as P

NX, NY, NZ = 4, 8, 8
MESH = pl.DeviceIdType.MESH
SEND_ORDER = (4, 3, 5, 2, 6, 1, 7)
WAIT_ORDER = (1, 7, 2, 6, 3, 5, 4)
BF16, F32 = jnp.bfloat16, jnp.float32


def remote(src, dst, send, recv, device):
    return pltpu.make_async_remote_copy(
        src_ref=src, dst_ref=dst, send_sem=send, recv_sem=recv, device_id=device, device_id_type=MESH
    )


def kernel(
    scale,
    hid, emb, head, lse, tok, tgt,
    out,
    H, E, HB, AUX, LP, RS, XF, G, P1, R1, S2, R2, R3, T, P4,
    loc_sem, sib_s, sib_r, head_s, head_r, rs_s, rs_r, ag_s, ag_r,
    p1_s, p1_r, p2_s, p2_r, p3_s, p3_r, p4_s, p4_r, fw_s, fw_r,
):
    x = lax.axis_index("vocab")
    d = lax.axis_index("dp")
    c, y, z = lax.rem(d, 2), lax.rem(d // 2, NY), d // (2 * NY)
    o = 1 - c
    m = 2 * x + c
    tokens = hid.shape[0]
    rows = head.shape[0]
    cols = hid.shape[1] // 2
    half = cols // 2

    def dev(px, py, pz, pc):
        return ((pz * NY + py) * 2 + pc, px)

    sibling = dev(x, y, z, o)
    ring = (lambda t: lax.rem(y + t, NY), lambda t: lax.rem(z + t, NZ))

    def ring_dev(h, p):
        return dev(x, p, z, c) if h == 0 else dev(x, y, p, c)

    def group_dev(p):
        return dev(p // 2, y, z, lax.rem(p, 2))

    pos = (y, z)
    pos2 = (z, y)

    def second_dev(h, px, p):
        return dev(px, y, p, c) if h == 0 else dev(px, p, z, c)

    own2 = tuple(p // 2 == x for p in pos2)

    mine = pl.ds(pl.multiple_of(c * tokens, tokens), tokens)
    theirs = pl.ds(pl.multiple_of(o * tokens, tokens), tokens)
    my_cols = pl.ds(pl.multiple_of(c * cols, cols), cols)
    their_cols = pl.ds(pl.multiple_of(o * cols, cols), cols)
    my_rows = pl.ds(pl.multiple_of(x * rows, rows), rows)
    locals_ = [
        pltpu.make_async_copy(head.at[:, pl.ds(pl.multiple_of(m * cols, cols), cols)], HB.at[my_rows, :], loc_sem.at[0]),
        pltpu.make_async_copy(hid.at[:, my_cols], H.at[mine, :], loc_sem.at[1]),
        pltpu.make_async_copy(emb.at[:, my_cols], E.at[mine, :], loc_sem.at[2]),
    ]
    for copy in locals_:
        copy.start()

    barrier = pltpu.get_barrier_semaphore()
    for t in range(1, 8):
        pl.semaphore_signal(barrier, inc=1, device_id=group_dev(lax.rem(m + t, 8)), device_id_type=MESH)
    for t in range(1, 8):
        for h in range(2):
            pl.semaphore_signal(barrier, inc=1, device_id=ring_dev(h, ring[h](t)), device_id_type=MESH)
    for h in range(2):
        for s in range(8):
            @pl.when(jnp.logical_not(own2[h] & (pos2[h] == s)))
            def _():
                pl.semaphore_signal(
                    barrier, inc=1, device_id=second_dev(h, pos2[h] // 2, s), device_id_type=MESH
                )

    AUX[mine_block(c), 0:1, :] = lse[...].reshape(1, 1, tokens)
    AUX[mine_block(c), 1:2, :] = tok[...].astype(F32).reshape(1, 1, tokens)
    AUX[mine_block(c), 2:3, :] = tgt[...].astype(F32).reshape(1, 1, tokens)

    pl.semaphore_wait(barrier, 37 - own2[0].astype(jnp.int32) - own2[1].astype(jnp.int32))

    head_copies = []
    for t in (2, 1, 3):
        px = lax.rem(x + t, NX)
        pcols = pl.ds(pl.multiple_of((2 * px + c) * cols, cols), cols)
        copy = remote(head.at[:, pcols], HB.at[my_rows, :], head_s.at[t], head_r.at[t], dev(px, y, z, c))
        copy.start()
        head_copies.append(copy)
    sib = [
        remote(AUX.at[c], AUX.at[c], sib_s.at[0], sib_r.at[0], sibling),
        remote(emb.at[:, their_cols], E.at[mine, :], sib_s.at[1], sib_r.at[1], sibling),
        remote(hid.at[:, their_cols], H.at[mine, :], sib_s.at[2], sib_r.at[2], sibling),
    ]
    for copy in sib:
        copy.start()

    sib_in = [
        remote(AUX.at[o], AUX.at[o], sib_s.at[0], sib_r.at[0], sibling),
        remote(E.at[theirs, :], E.at[theirs, :], sib_s.at[1], sib_r.at[1], sibling),
        remote(H.at[theirs, :], H.at[theirs, :], sib_s.at[2], sib_r.at[2], sibling),
    ]
    sib_in[0].wait_recv()
    sib_in[1].wait_recv()
    locals_[2].wait()
    vocab = NX * rows
    order = lax.broadcasted_iota(jnp.int32, (vocab, tokens), 0)
    ordered = rows * ((order // 4) % 4) + 4 * (order // 16) + order % 4
    ordered = ordered.astype(F32)
    picks = jnp.concatenate(
        [jnp.where(AUX[k, 1:2, :] == ordered, 1.0, 0.0).astype(BF16) for k in range(2)], axis=1
    )
    step = half // 3
    for k in range(6):
        s = slice(k * step, (k + 1) * step)
        G[:, s] = jnp.dot(picks, E[:, s], preferred_element_type=F32)

    sib_in[2].wait_recv()
    locals_[1].wait()
    locals_[0].wait()
    for t in (1, 3, 2):
        src_rows = pl.ds(pl.multiple_of(lax.rem(x + NX - t, NX) * rows, rows), rows)
        remote(HB.at[src_rows, :], HB.at[src_rows, :], head_s.at[t], head_r.at[t], sibling).wait_recv()
    LP[...] = lax.dot_general(HB[...], H[...], (((1,), (1,)), ((), ())), preferred_element_type=F32)

    for t in SEND_ORDER:
        p = lax.rem(m + t, 8)
        remote(
            LP.at[pl.ds(pl.multiple_of(p * 16, 16), 16), :], RS.at[m], rs_s.at[t], rs_r.at[t], group_dev(p)
        ).start()
    my16 = pl.ds(pl.multiple_of(m * 16, 16), 16)
    logits = LP[my16, :]
    for t in WAIT_ORDER:
        p = lax.rem(m + 8 - t, 8)
        remote(RS.at[p], RS.at[p], rs_s.at[t], rs_r.at[t], sibling).wait_recv()
        logits = logits + RS[p]
    XF[my16, :] = jnp.exp(logits)
    for t in SEND_ORDER:
        p = lax.rem(m + t, 8)
        remote(XF.at[my16, :], XF.at[my16, :], ag_s.at[t], ag_r.at[t], group_dev(p)).start()
    natural = lax.broadcasted_iota(jnp.int32, (vocab, tokens), 0).astype(F32)
    swap_r = lax.broadcasted_iota(jnp.int32, (vocab, vocab), 0)
    swap_c = lax.broadcasted_iota(jnp.int32, (vocab, vocab), 1)
    swap = jnp.where(rows * ((swap_r // 4) % 4) + 4 * (swap_r // 16) + swap_r % 4 == swap_c, 1.0, 0.0).astype(BF16)
    for t in WAIT_ORDER:
        p = lax.rem(m + 8 - t, 8)
        p16 = pl.ds(pl.multiple_of(p * 16, 16), 16)
        remote(XF.at[p16, :], XF.at[p16, :], ag_s.at[t], ag_r.at[t], sibling).wait_recv()
    parts = []
    for k in range(2):
        ex = XF[:, k * tokens:(k + 1) * tokens]
        denominator = jnp.exp(AUX[k, 0:1, :]) + jnp.sum(ex, axis=0, keepdims=True)
        coefficients = ex / denominator - jnp.where(AUX[k, 2:3, :] == natural, 1.0, 0.0)
        parts.append(coefficients.astype(BF16))
    coef = jnp.concatenate(parts, axis=1)
    coef = jnp.dot(swap, coef, preferred_element_type=F32).astype(BF16)

    for h in range(2):
        for k in range(3):
            s = slice(h * half + k * step, h * half + (k + 1) * step)
            g = (G[:, s] + jnp.dot(coef, H[:, s], preferred_element_type=F32)) * scale
            G[:, s] = g
            P1[h, :, :, k * step:(k + 1) * step] = g.astype(BF16).reshape(8, 16, step)
        for t in SEND_ORDER:
            p = ring[h](t)
            remote(P1.at[h, p], R1.at[h, pos[h]], p1_s.at[h, t], p1_r.at[h, t], ring_dev(h, p)).start()

    for h in range(2):
        acc = G[pl.ds(pl.multiple_of(pos[h] * 16, 16), 16), h * half:(h + 1) * half]
        for t in WAIT_ORDER:
            p = ring[h](8 - t)
            remote(R1.at[h, p], R1.at[h, p], p1_s.at[h, t], p1_r.at[h, t], sibling).wait_recv()
            acc = acc + R1[h, p].astype(F32)
        for q in range(8):
            S2[h, q] = acc[2 * q:2 * q + 2, :]
        for q in range(8):
            target = 2 * x + q % 2
            is_self = (x == q // 2) & (target == pos2[h])

            @pl.when(jnp.logical_not(is_self))
            def _():
                remote(
                    S2.at[h, q], R2.at[h, pos2[h]], p2_s.at[h, q], p2_r.at[h, pos2[h]],
                    second_dev(h, q // 2, target),
                ).start()

            @pl.when(is_self)
            def _():
                R2[h, pos2[h]] = S2[h, q]

    for h in range(2):
        total = jnp.zeros((2, half), F32)
        for s in range(8):
            @pl.when(jnp.logical_not(own2[h] & (pos2[h] == s)))
            def _():
                remote(R2.at[h, s], R2.at[h, s], p2_s.at[h, s], p2_r.at[h, s], sibling).wait_recv()
        for s in range(8):
            total = total + R2[h, s]
        R3[h, pos2[h]] = total
        for t in SEND_ORDER:
            p = ring[1 - h](t)
            remote(
                R3.at[h, pos2[h]], R3.at[h, pos2[h]], p3_s.at[h, t], p3_r.at[h, t], ring_dev(1 - h, p)
            ).start()

    for h in range(2):
        for t in WAIT_ORDER:
            p = ring[1 - h](8 - t)
            remote(R3.at[h, p], R3.at[h, p], p3_s.at[h, t], p3_r.at[h, t], sibling).wait_recv()
        for k in range(8):
            T[h, 2 * k:2 * k + 2, :] = R3[h, k]
        P4[h] = T[h].astype(BF16)
        for t in SEND_ORDER:
            p = ring[h](t)
            remote(P4.at[h], out.at[h, c, pos[h]], p4_s.at[h, t], p4_r.at[h, t], ring_dev(h, p)).start()
        remote(P4.at[h], out.at[h, c, pos[h]], fw_s.at[h, 0], fw_r.at[h, 0], sibling).start()
        pltpu.make_async_copy(P4.at[h], out.at[h, c, pos[h]], loc_sem.at[3 + h]).start()

    for t in WAIT_ORDER:
        for h in range(2):
            p = ring[h](8 - t)
            slot = out.at[h, c, p]
            remote(slot, slot, p4_s.at[h, t], p4_r.at[h, t], sibling).wait_recv()
            remote(slot, slot, fw_s.at[h, t], fw_r.at[h, t], sibling).start()

    for copy in head_copies + sib:
        copy.wait_send()
    for t in SEND_ORDER:
        remote(RS.at[0], RS.at[0], rs_s.at[t], rs_r.at[t], sibling).wait_send()
        remote(XF.at[my16, :], XF.at[my16, :], ag_s.at[t], ag_r.at[t], sibling).wait_send()
        for h in range(2):
            remote(P1.at[h, 0], R1.at[h, 0], p1_s.at[h, t], p1_r.at[h, t], sibling).wait_send()
            remote(R3.at[h, 0], R3.at[h, 0], p3_s.at[h, t], p3_r.at[h, t], sibling).wait_send()
            remote(P4.at[h], P4.at[h], p4_s.at[h, t], p4_r.at[h, t], sibling).wait_send()
    for h in range(2):
        for q in range(8):
            is_self = (x == q // 2) & (2 * x + q % 2 == pos2[h])

            @pl.when(jnp.logical_not(is_self))
            def _():
                remote(S2.at[h, q], S2.at[h, q], p2_s.at[h, q], p2_r.at[h, q], sibling).wait_send()
        pltpu.make_async_copy(P4.at[h], out.at[h, c, pos[h]], loc_sem.at[3 + h]).wait()
        for t in range(8):
            p = ring[h](8 - t)
            slot = out.at[h, o, p]
            remote(slot, slot, fw_s.at[h, t], fw_r.at[h, t], sibling).wait()


def mine_block(c):
    return pl.ds(c, 1)


def arrange(pieces, result):
    _, _, _, _, half = pieces.shape
    for h in range(2):
        for c in range(2):
            for g in range(2):
                group = [pieces[h, c, 4 * g + j].astype(F32) for j in range(4)]
                for x in range(NX):
                    block = jnp.concatenate([p[4 * x:4 * x + 4, :] for p in group], axis=0)
                    start = (2 * x + c) * 2 * half + h * half
                    result[16 * g:16 * g + 16, start:start + half] = block.astype(BF16)


def local(hidden, embed_cot, head_block, lse_rest, token_ids, target_ids):
    tokens, width = hidden.shape
    rows, model = head_block.shape
    cols, half, vocab = width // 2, width // 4, rows * NX
    scale = math.sqrt(vocab / (tokens * lax.axis_size("dp")))
    hbm = pl.BlockSpec(memory_space=pl.ANY)
    vmem = pl.BlockSpec(memory_space=pltpu.VMEM)
    dma = pltpu.SemaphoreType.DMA
    pieces = pl.pallas_call(
        functools.partial(kernel, scale),
        out_shape=jax.ShapeDtypeStruct((2, 2, 8, 16, half), BF16),
        in_specs=[hbm, hbm, hbm, vmem, vmem, vmem],
        out_specs=hbm,
        scratch_shapes=[
            pltpu.VMEM((2 * tokens, cols), BF16),
            pltpu.VMEM((2 * tokens, cols), BF16),
            pltpu.VMEM((vocab, cols), BF16),
            pltpu.VMEM((2, 8, tokens), F32),
            pltpu.VMEM((vocab, 2 * tokens), F32),
            pltpu.VMEM((8, 16, 2 * tokens), F32),
            pltpu.VMEM((vocab, 2 * tokens), F32),
            pltpu.VMEM((vocab, cols), F32),
            pltpu.VMEM((2, 8, 16, half), BF16),
            pltpu.VMEM((2, 8, 16, half), BF16),
            pltpu.VMEM((2, 8, 2, half), F32),
            pltpu.VMEM((2, 8, 2, half), F32),
            pltpu.VMEM((2, 8, 2, half), F32),
            pltpu.VMEM((2, 16, half), F32),
            pltpu.VMEM((2, 16, half), BF16),
            dma((5,)),
            dma((3,)), dma((3,)),
            dma((4,)), dma((4,)),
            dma((8,)), dma((8,)),
            dma((8,)), dma((8,)),
            dma((2, 8)), dma((2, 8)),
            dma((2, 8)), dma((2, 8)),
            dma((2, 8)), dma((2, 8)),
            dma((2, 8)), dma((2, 8)),
            dma((2, 8)), dma((2, 8)),
        ],
        compiler_params=pltpu.CompilerParams(
            collective_id=0, has_side_effects=True, vmem_limit_bytes=40 * 1024 * 1024
        ),
        name="exchange",
    )(
        hidden, embed_cot, head_block,
        lse_rest.reshape(1, tokens), token_ids.reshape(1, tokens), target_ids.reshape(1, tokens),
    )
    return pl.pallas_call(
        arrange,
        out_shape=jax.ShapeDtypeStruct((rows, model), BF16),
        in_specs=[vmem],
        out_specs=vmem,
        compiler_params=pltpu.CompilerParams(vmem_limit_bytes=40 * 1024 * 1024),
        name="arrange",
    )(pieces)


def solution(mesh):
    return jax.shard_map(
        local,
        mesh=mesh,
        in_specs=(P("dp", "vocab"), P("dp", "vocab"), P("vocab", None), P("dp"), P("dp"), P("dp")),
        out_specs=P("vocab", None),
        check_vma=False,
    )
```

time: 452 us -> 72.2 us (0.16)
  waiting for transfers between devices: 404 us -> 0 us
  Pallas kernels: 0 us -> 66.2 us
  between operations: 13.1 us -> 0.02 us
  matrix products: 11.8 us -> 0 us
  local copies, waits for them, and re-layouts: 15.3 us -> 5.77 us
  blocking collectives: 6.68 us -> 0 us
    unnamed x5 -> x0, waiting for transfers between devices: 206 us -> none
    all_gather x3 -> x0, waiting for transfers between devices: 198 us -> none  [the longest x1 87 us: replica_sum(): return lax.all_gather(shares, 'dp', axis=1, tiled=True)]
    pallas_call x0 -> x2, Pallas kernels: none -> 66.2 us  [the longest x1 64.9 us: local(): pl.pallas_call(functools.partial(kernel, scale), out_shape=jax.ShapeDtype...]
    dot_general x3 -> x0, matrix products: 11.8 us -> none  [the longest x1 4.57 us: gradient_terms(): jnp.dot(picks.T, cotangents, preferred_element_type=jnp.float32)]
    unnamed x7 -> x12, local copies, waits for them, and re-layouts: 12.5 us -> 5.77 us
    psum x1 -> x0, blocking collectives: 6.68 us -> none  [local(): block_sum = lax.psum(jnp.sum(exponent, axis=1), 'vocab')]
  transfers between devices with their start and end apart: 4 -> 0, of which waited for: 4 -> 0; matrix products, arithmetic and copies ran while one was open for 2% -> 0% of each run, Pallas kernels for 0% -> 0%
where the time goes in v1:
time: 72.2 us; the launch traced here: 72 us
  Pallas kernels  66.2 us (92%)
  local copies, waits for them, and re-layouts  5.77 us (8%)
    pallas_call x1, Pallas kernels, local(): pl.pallas_call(functools.partial(kernel, scale), out_shape=jax.ShapeDtype...  64.9 us
    unnamed x12, local copies, waits for them, and re-layouts  5.77 us

profile of v1, /device:TPU:1, one launch (start us, length us, event | category | flops | bytes accessed | tf_op | source)
XLA Modules:
  0.0 72.0 jit_solution(489523054867207753)
XLA Ops:
  0.0 0.0 copy-start
  0.0 1.3 %copy-done = bf16[128,4608]{1,0:T(8,128)(2,1)S(1)} copy-done((bf16[128,4608]{1,0:T(8,128)(2,1)S(1)}, bf16[128,4608]{1,0:T(8,128)(2,1)}, u32[]{:S(2)}) %copy-start) | copy-done | bytes 1179672
  1.3 0.0 copy-start.1
  1.3 1.3 %copy-done.1 = bf16[128,4608]{1,0:T(8,128)(2,1)S(1)} copy-done((bf16[128,4608]{1,0:T(8,128)(2,1)S(1)}, bf16[128,4608]{1,0:T(8,128)(2,1)}, u32[]{:S(2)}) %copy-start.1) | copy-done | bytes 1179672
  2.5 0.0 copy-start.2
  2.5 1.3 %copy-done.2 = bf16[32,18432]{1,0:T(8,128)(2,1)S(1)} copy-done((bf16[32,18432]{1,0:T(8,128)(2,1)S(1)}, bf16[32,18432]{1,0:T(8,128)(2,1)}, u32[]{:S(2)}) %copy-start.2) | copy-done | bytes 1179672
  3.8 0.0 copy-start.3
  3.8 0.7 copy-done.3
  4.5 0.0 copy-start.4
  4.5 0.7 copy-done.4
  5.1 0.0 copy-start.5
  5.1 0.7 copy-done.5
  5.8 64.9 %exchange.1.pieces = bf16[2,2,8,16,1152]{4,3,2,1,0:T(8,128)(2,1)S(1)} custom-call(bf16[128,4608]{1,0:T(8,128)(2,1)S(1)} %copy-done, bf16[128,4608]{1,0:T(8,128)(2,1)S(1)} %copy-done.1, bf16[32,18432]{1,0:T(8,128)(2,1)S(1)} %copy-done.2, f32[1,128]{1,0:T(1,128)S(1)} %bitcast.3, s32[1,128]{1,0:T(1,128)S(1)} %bitcast.4, s32[1,128]{1,0:T(1,128)S(1)} %bitcast.5), custom_call_target="tpu_custom_call" | custom-call | tf_op jit(solution)/shard_map/exchange/pallas_call | solution.py:285
  70.7 1.3 %arrange.1 = bf16[32,18432]{1,0:T(8,128)(2,1)} custom-call(bf16[2,2,8,16,1152]{4,3,2,1,0:T(8,128)(2,1)S(1)} %exchange.1.pieces), custom_call_target="tpu_custom_call" | custom-call | tf_op jit(solution)/shard_map/arrange/pallas_call | solution.py:325
Async XLA Ops:
  0.0 1.3 %copy-start = (bf16[128,4608]{1,0:T(8,128)(2,1)S(1)}, bf16[128,4608]{1,0:T(8,128)(2,1)}, u32[]{:S(2)}) copy-start(bf16[128,4608]{1,0:T(8,128)(2,1)} %hid.1) | copy-start | bytes 3538948
  1.3 1.3 %copy-start.1 = (bf16[128,4608]{1,0:T(8,128)(2,1)S(1)}, bf16[128,4608]{1,0:T(8,128)(2,1)}, u32[]{:S(2)}) copy-start(bf16[128,4608]{1,0:T(8,128)(2,1)} %emb.1) | copy-start | bytes 3538948
  2.5 1.3 %copy-start.2 = (bf16[32,18432]{1,0:T(8,128)(2,1)S(1)}, bf16[32,18432]{1,0:T(8,128)(2,1)}, u32[]{:S(2)}) copy-start(bf16[32,18432]{1,0:T(8,128)(2,1)} %head.1) | copy-start | bytes 3538948
  3.8 0.7 copy-start.3
  4.5 0.7 copy-start.4
  5.1 0.7 copy-start.5

commit v2 on v1

v2 whole, which is shorter than its diff:
```python
import functools
import math

import jax
import jax.numpy as jnp
from jax import lax
from jax.experimental import pallas as pl
from jax.experimental.pallas import tpu as pltpu
from jax.sharding import PartitionSpec as P

NX, NY, NZ = 4, 8, 8
MESH = pl.DeviceIdType.MESH
SEND_ORDER = (4, 3, 5, 2, 6, 1, 7)
WAIT_ORDER = (1, 7, 2, 6, 3, 5, 4)
CHUNKS = 3
BF16, F32 = jnp.bfloat16, jnp.float32


def remote(src, dst, send, recv, device):
    return pltpu.make_async_remote_copy(
        src_ref=src, dst_ref=dst, send_sem=send, recv_sem=recv, device_id=device, device_id_type=MESH
    )


def kernel(
    scale,
    hid, emb, head, lse, tok, tgt,
    out,
    H, E, HB, LSE, TOK, TGT, LP, RS, XF, G, P1, R1, S2, R2, R3, T, P4,
    loc_sem, out_sem, sib_s, sib_r, head_s, head_r, rs_s, rs_r, ag_s, ag_r,
    p1_s, p1_r, p2_s, p2_r, p3_s, p3_r, p4_s, p4_r, fw_s, fw_r,
):
    x = lax.axis_index("vocab")
    d = lax.axis_index("dp")
    c, y, z = lax.rem(d, 2), lax.rem(d // 2, NY), d // (2 * NY)
    o = 1 - c
    m = 2 * x + c
    tokens = hid.shape[0]
    rows = head.shape[0]
    cols = hid.shape[1] // 2
    half = cols // 2

    def dev(px, py, pz, pc):
        return ((pz * NY + py) * 2 + pc, px)

    sibling = dev(x, y, z, o)
    ring = (lambda t: lax.rem(y + t, NY), lambda t: lax.rem(z + t, NZ))

    def ring_dev(h, p):
        return dev(x, p, z, c) if h == 0 else dev(x, y, p, c)

    def group_dev(p):
        return dev(p // 2, y, z, lax.rem(p, 2))

    pos = (y, z)
    pos2 = (z, y)

    def second_dev(h, px, p):
        return dev(px, y, p, c) if h == 0 else dev(px, p, z, c)

    source = tuple(lax.rem(p // 2 + NX - x, NX) for p in pos2)
    own2 = tuple(p == x for p in source)

    mine = pl.ds(pl.multiple_of(c * tokens, tokens), tokens)
    theirs = pl.ds(pl.multiple_of(o * tokens, tokens), tokens)
    my_cols = pl.ds(pl.multiple_of(c * cols, cols), cols)
    their_cols = pl.ds(pl.multiple_of(o * cols, cols), cols)
    my_rows = pl.ds(pl.multiple_of(x * rows, rows), rows)
    locals_ = [
        pltpu.make_async_copy(head.at[:, pl.ds(pl.multiple_of(m * cols, cols), cols)], HB.at[my_rows, :], loc_sem.at[0]),
        pltpu.make_async_copy(hid.at[:, my_cols], H.at[mine, :], loc_sem.at[1]),
        pltpu.make_async_copy(emb.at[:, my_cols], E.at[mine, :], loc_sem.at[2]),
        pltpu.make_async_copy(tok, TOK.at[c], loc_sem.at[3]),
        pltpu.make_async_copy(lse, LSE.at[c], loc_sem.at[4]),
        pltpu.make_async_copy(tgt, TGT.at[c], loc_sem.at[5]),
    ]
    for copy in locals_:
        copy.start()

    barrier = pltpu.get_barrier_semaphore()
    for t in range(1, 8):
        pl.semaphore_signal(barrier, inc=1, device_id=group_dev(lax.rem(m + t, 8)), device_id_type=MESH)
    for t in range(1, 8):
        for h in range(2):
            pl.semaphore_signal(barrier, inc=1, device_id=ring_dev(h, ring[h](t)), device_id_type=MESH)
    for h in range(2):
        for s in range(8):
            @pl.when(jnp.logical_not(own2[h] & (pos2[h] == s)))
            def _():
                pl.semaphore_signal(
                    barrier, inc=1, device_id=second_dev(h, source[h], s), device_id_type=MESH
                )

    pl.semaphore_wait(barrier, 37 - own2[0].astype(jnp.int32) - own2[1].astype(jnp.int32))

    for t in (2, 1, 3):
        px = lax.rem(x + t, NX)
        pcols = pl.ds(pl.multiple_of((2 * px + c) * cols, cols), cols)
        copy = remote(head.at[:, pcols], HB.at[my_rows, :], head_s, head_r, dev(px, y, z, c))
        copy.start()
    sib = [
        remote(tok, TOK.at[c], sib_s.at[0], sib_r.at[0], sibling),
        remote(lse, LSE.at[c], sib_s.at[3], sib_r.at[3], sibling),
        remote(tgt, TGT.at[c], sib_s.at[4], sib_r.at[4], sibling),
        remote(emb.at[:, their_cols], E.at[mine, :], sib_s.at[1], sib_r.at[1], sibling),
        remote(hid.at[:, their_cols], H.at[mine, :], sib_s.at[2], sib_r.at[2], sibling),
    ]
    for copy in sib:
        copy.start()

    sib_in = [
        remote(TOK.at[o], TOK.at[o], sib_s.at[0], sib_r.at[0], sibling),
        remote(E.at[theirs, :], E.at[theirs, :], sib_s.at[1], sib_r.at[1], sibling),
        remote(H.at[theirs, :], H.at[theirs, :], sib_s.at[2], sib_r.at[2], sibling),
        remote(LSE.at[o], LSE.at[o], sib_s.at[3], sib_r.at[3], sibling),
        remote(TGT.at[o], TGT.at[o], sib_s.at[4], sib_r.at[4], sibling),
    ]
    sib_in[0].wait_recv()
    sib_in[1].wait_recv()
    locals_[2].wait()
    locals_[3].wait()
    vocab = NX * rows
    order = lax.broadcasted_iota(jnp.int32, (vocab, tokens), 0)
    ordered = rows * ((order // 4) % 4) + 4 * (order // 16) + order % 4
    picks = jnp.concatenate(
        [jnp.where(TOK[k] == ordered, 1.0, 0.0).astype(BF16) for k in range(2)], axis=1
    )
    step = half // 3
    for k in range(6):
        s = slice(k * step, (k + 1) * step)
        G[:, s] = jnp.dot(picks, E[:, s], preferred_element_type=F32)

    for copy in sib_in[2:]:
        copy.wait_recv()
    locals_[4].wait()
    locals_[5].wait()
    locals_[1].wait()
    locals_[0].wait()
    heads = remote(HB.at[:(NX - 1) * rows, :], HB.at[:(NX - 1) * rows, :], head_s, head_r, sibling)
    heads.wait_recv()
    LP[...] = lax.dot_general(HB[...], H[...], (((1,), (1,)), ((), ())), preferred_element_type=F32)

    for t in SEND_ORDER:
        p = lax.rem(m + t, 8)
        remote(
            LP.at[pl.ds(pl.multiple_of(p * 16, 16), 16), :], RS.at[m], rs_s, rs_r, group_dev(p)
        ).start()
    my16 = pl.ds(pl.multiple_of(m * 16, 16), 16)
    logits = LP[my16, :]
    remote(RS.at[:7], RS.at[:7], rs_s, rs_r, sibling).wait_recv()
    for t in SEND_ORDER:
        logits = logits + RS[lax.rem(m + t, 8)]
    XF[my16, :] = jnp.exp(logits)
    for t in SEND_ORDER:
        p = lax.rem(m + t, 8)
        remote(XF.at[my16, :], XF.at[my16, :], ag_s, ag_r, group_dev(p)).start()
    natural = lax.broadcasted_iota(jnp.int32, (vocab, tokens), 0)
    swap_r = lax.broadcasted_iota(jnp.int32, (vocab, vocab), 0)
    swap_c = lax.broadcasted_iota(jnp.int32, (vocab, vocab), 1)
    swap = jnp.where(rows * ((swap_r // 4) % 4) + 4 * (swap_r // 16) + swap_r % 4 == swap_c, 1.0, 0.0).astype(BF16)
    remote(XF.at[:7 * 16, :], XF.at[:7 * 16, :], ag_s, ag_r, sibling).wait_recv()
    parts = []
    for k in range(2):
        ex = XF[:, k * tokens:(k + 1) * tokens]
        denominator = jnp.exp(LSE[k]) + jnp.sum(ex, axis=0, keepdims=True)
        coefficients = ex / denominator - jnp.where(TGT[k] == natural, 1.0, 0.0)
        parts.append(coefficients.astype(BF16))
    coef = jnp.concatenate(parts, axis=1)
    coef = jnp.dot(swap, coef, preferred_element_type=F32).astype(BF16)

    chunks = [[(h, k) for h in range(2)] for k in range(CHUNKS)]
    width = half // CHUNKS

    def span(h, k):
        return slice(h * half + k * width, h * half + (k + 1) * width)

    def first(q):
        h, k = q
        s = span(h, k)
        g = (G[:, s] + jnp.dot(coef, H[:, s], preferred_element_type=F32)) * scale
        G[:, s] = g
        P1[h, k] = g.astype(BF16).reshape(8, 16, width)
        for t in SEND_ORDER:
            p = ring[h](t)
            remote(
                P1.at[h, k, p], R1.at[h, k, pos[h]], p1_s.at[h, k], p1_r.at[h, k], ring_dev(h, p)
            ).start()

    def second_waits(q, wait):
        h, k = q
        for n, here in ((7, own2[h]), (8, jnp.logical_not(own2[h]))):
            copy = remote(R2.at[h, k, :n], R2.at[h, k, :n], p2_s.at[h, k], p2_r.at[h, k], sibling)
            pl.when(here)(lambda: wait(copy))

    def second(q):
        h, k = q
        acc = G[pl.ds(pl.multiple_of(pos[h] * 16, 16), 16), span(h, k)]
        remote(R1.at[h, k, :7], R1.at[h, k, :7], p1_s.at[h, k], p1_r.at[h, k], sibling).wait_recv()
        for t in SEND_ORDER:
            acc = acc + R1[h, k, ring[h](t)].astype(F32)
        for i in range(8):
            S2[h, k, i] = acc[2 * i:2 * i + 2, :]
        for r in range(8):
            px = lax.rem(x + r // 2, NX)
            target = 2 * lax.rem(x + px, NX) + r % 2
            i = 2 * px + r % 2
            copy = remote(
                S2.at[h, k, i], R2.at[h, k, pos2[h]], p2_s.at[h, k], p2_r.at[h, k], second_dev(h, px, target)
            )
            if r > 1:
                copy.start()
            else:
                is_self = target == pos2[h]
                pl.when(jnp.logical_not(is_self))(copy.start)

                @pl.when(is_self)
                def _():
                    R2[h, k, pos2[h]] = S2[h, k, i]

    def third(q):
        h, k = q
        second_waits(q, lambda copy: copy.wait_recv())
        total = R2[h, k, 0]
        for s in range(1, 8):
            total = total + R2[h, k, s]
        R3[h, k, pos2[h]] = total
        for t in SEND_ORDER:
            p = ring[1 - h](t)
            remote(
                R3.at[h, k, pos2[h]], R3.at[h, k, pos2[h]], p3_s.at[h, k], p3_r.at[h, k],
                ring_dev(1 - h, p),
            ).start()

    def fourth(q):
        h, k = q
        remote(R3.at[h, k, :7], R3.at[h, k, :7], p3_s.at[h, k], p3_r.at[h, k], sibling).wait_recv()
        for i in range(8):
            T[h, k, 2 * i:2 * i + 2, :] = R3[h, k, i]
        P4[h, k] = T[h, k].astype(BF16)
        slot = out.at[h, c, k, pos[h]]
        for t in SEND_ORDER:
            p = ring[h](t)
            remote(P4.at[h, k], slot, p4_s.at[h, k], p4_r.at[h, k, t], ring_dev(h, p)).start()
        remote(P4.at[h, k], slot, fw_s.at[h, k], fw_r.at[h, k], sibling).start()
        pltpu.make_async_copy(P4.at[h, k], slot, out_sem.at[h, k]).start()

    def fifth(q):
        h, k = q
        for t in WAIT_ORDER:
            slot = out.at[h, c, k, ring[h](8 - t)]
            remote(slot, slot, p4_s.at[h, k], p4_r.at[h, k, t], sibling).wait_recv()
            remote(slot, slot, fw_s.at[h, k], fw_r.at[h, k], sibling).start()

    for step in (first, second, third, fourth, fifth):
        for group in chunks:
            for q in group:
                step(q)

    heads.wait_send()
    for copy in sib:
        copy.wait_send()
    remote(RS.at[:7], RS.at[:7], rs_s, rs_r, sibling).wait_send()
    remote(XF.at[:7 * 16, :], XF.at[:7 * 16, :], ag_s, ag_r, sibling).wait_send()
    for h, k in [q for group in chunks for q in group]:
        remote(P1.at[h, k, :7], P1.at[h, k, :7], p1_s.at[h, k], p1_r.at[h, k], sibling).wait_send()
        remote(R3.at[h, k, :7], R3.at[h, k, :7], p3_s.at[h, k], p3_r.at[h, k], sibling).wait_send()
        remote(P1.at[h, k, :7], P1.at[h, k, :7], p4_s.at[h, k], p4_r.at[h, k, 0], sibling).wait_send()
        second_waits((h, k), lambda copy: copy.wait_send())
        pltpu.make_async_copy(P4.at[h, k], out.at[h, c, k, pos[h]], out_sem.at[h, k]).wait()
        remote(out.at[h, o, k], out.at[h, o, k], fw_s.at[h, k], fw_r.at[h, k], sibling).wait()


def arrange(pieces, result, held, made, in_sem, out_sem):
    width = pieces.shape[-1]
    half = CHUNKS * width
    me = lax.axis_index("vocab")
    places = [(h, c, k) for k in range(CHUNKS) for h in range(2) for c in range(2)]
    loads = [pltpu.make_async_copy(pieces.at[q], held.at[q], in_sem.at[q]) for q in places]
    for copy in loads:
        copy.start()
    stores = []
    for (h, c, k), load in zip(places, loads):
        load.wait()
        for g in range(2):
            group = [held[h, c, k, 4 * g + j].astype(F32) for j in range(4)]
            for x in range(NX):
                block = jnp.concatenate([p[4 * x:4 * x + 4, :] for p in group], axis=0)
                start = (2 * x + c) * 2 * half + h * half + k * width
                made[16 * g:16 * g + 16, start:start + width] = block.astype(BF16)
        for x in range(NX):
            start = (2 * x + c) * 2 * half + h * half + k * width
            place = (2 * lax.rem(x + NX - me, NX) + c) * 2 * half + h * half + k * width
            place = pl.ds(pl.multiple_of(place, 128), width)
            stores.append(
                pltpu.make_async_copy(made.at[:, pl.ds(start, width)], result.at[:, place], out_sem.at[h, c, k, x])
            )
            stores[-1].start()
    for copy in stores:
        copy.wait()


def local(hidden, embed_cot, head_block, lse_rest, token_ids, target_ids):
    tokens, width = hidden.shape
    rows, model = head_block.shape
    cols, width_, vocab = width // 2, width // 4 // CHUNKS, rows * NX
    scale = math.sqrt(vocab / (tokens * lax.axis_size("dp")))
    hbm = pl.BlockSpec(memory_space=pl.ANY)
    dma = pltpu.SemaphoreType.DMA
    pieces = pl.pallas_call(
        functools.partial(kernel, scale),
        out_shape=jax.ShapeDtypeStruct((2, 2, CHUNKS, 8, 16, width_), BF16),
        in_specs=[hbm] * 6,
        out_specs=hbm,
        scratch_shapes=[
            pltpu.VMEM((2 * tokens, cols), BF16),
            pltpu.VMEM((2 * tokens, cols), BF16),
            pltpu.VMEM((vocab, cols), BF16),
            pltpu.VMEM((2, 1, tokens), F32),
            pltpu.VMEM((2, 1, tokens), jnp.int32),
            pltpu.VMEM((2, 1, tokens), jnp.int32),
            pltpu.VMEM((vocab, 2 * tokens), F32),
            pltpu.VMEM((8, 16, 2 * tokens), F32),
            pltpu.VMEM((vocab, 2 * tokens), F32),
            pltpu.VMEM((vocab, cols), F32),
            pltpu.VMEM((2, CHUNKS, 8, 16, width_), BF16),
            pltpu.VMEM((2, CHUNKS, 8, 16, width_), BF16),
            pltpu.VMEM((2, CHUNKS, 8, 2, width_), F32),
            pltpu.VMEM((2, CHUNKS, 8, 2, width_), F32),
            pltpu.VMEM((2, CHUNKS, 8, 2, width_), F32),
            pltpu.VMEM((2, CHUNKS, 16, width_), F32),
            pltpu.VMEM((2, CHUNKS, 16, width_), BF16),
            dma((6,)),
            dma((2, CHUNKS)),
            dma((5,)), dma((5,)),
            dma, dma,
            dma, dma,
            dma, dma,
            dma((2, CHUNKS)), dma((2, CHUNKS)),
            dma((2, CHUNKS)), dma((2, CHUNKS)),
            dma((2, CHUNKS)), dma((2, CHUNKS)),
            dma((2, CHUNKS)), dma((2, CHUNKS, 8)),
            dma((2, CHUNKS)), dma((2, CHUNKS)),
        ],
        compiler_params=pltpu.CompilerParams(
            collective_id=0, has_side_effects=True, vmem_limit_bytes=60 * 1024 * 1024
        ),
        name="exchange",
    )(
        hidden, embed_cot, head_block,
        lse_rest.reshape(1, tokens), token_ids.reshape(1, tokens), target_ids.reshape(1, tokens),
    )
    return pl.pallas_call(
        arrange,
        out_shape=jax.ShapeDtypeStruct((rows, model), BF16),
        in_specs=[hbm],
        out_specs=hbm,
        scratch_shapes=[
            pltpu.VMEM((2, 2, CHUNKS, 8, 16, width_), BF16),
            pltpu.VMEM((rows, model), BF16),
            dma((2, 2, CHUNKS)),
            dma((2, 2, CHUNKS, NX)),
        ],
        compiler_params=pltpu.CompilerParams(vmem_limit_bytes=60 * 1024 * 1024),
        name="arrange",
    )(pieces)


def solution(mesh):
    return jax.shard_map(
        local,
        mesh=mesh,
        in_specs=(P("dp", "vocab"), P("dp", "vocab"), P("vocab", None), P("dp"), P("dp"), P("dp")),
        out_specs=P("vocab", None),
        check_vma=False,
    )
```

time: 72.2 us -> 64.1 us (0.89)
  local copies, waits for them, and re-layouts: 5.77 us -> 0 us
  Pallas kernels: 66.2 us -> 63.9 us
    unnamed x12 -> x0, local copies, waits for them, and re-layouts: 5.77 us -> none
    pallas_call x1, Pallas kernels: 64.9 us -> 61.4 us  [local(): pl.pallas_call(functools.partial(kernel, scale), out_shape=jax.ShapeDtype...]
    pallas_call x1, Pallas kernels: 1.29 us -> 2.53 us  [local(): pl.pallas_call(arrange, out_shape=jax.ShapeDtypeStruct((rows, model), BF1...]
where the time goes in v2:
time: 64.1 us; the launch traced here: 63.9 us
  Pallas kernels  63.9 us (100%)
    pallas_call x1, Pallas kernels, local(): pl.pallas_call(functools.partial(kernel, scale), out_shape=jax.ShapeDtype...  61.4 us
    pallas_call x1, Pallas kernels, local(): pl.pallas_call(arrange, out_shape=jax.ShapeDtypeStruct((rows, model), BF1...  2.53 us

profile of v2, /device:TPU:1, one launch (start us, length us, event | category | flops | bytes accessed | tf_op | source)
XLA Modules:
  0.0 63.9 jit_solution(9458315550601710776)
XLA Ops:
  0.0 61.4 %exchange.1.pieces = bf16[2,2,3,8,16,384]{5,4,3,2,1,0:T(8,128)(2,1)} custom-call(bf16[128,4608]{1,0:T(8,128)(2,1)} %hid.1, bf16[128,4608]{1,0:T(8,128)(2,1)} %emb.1, bf16[32,18432]{1,0:T(8,128)(2,1)} %head.1, f32[1,128]{1,0:T(1,128)} %bitcast.3, s32[1,128]{1,0:T(1,128)} %bitcast.4, s32[1,128]{1,0:T(1,128)} %bitcast.5), custom_call_target="tpu_custom_call" | custom-call | tf_op jit(solution)/shard_map/exchange/pallas_call | solution.py:309
  61.4 2.5 %arrange.1 = bf16[32,18432]{1,0:T(8,128)(2,1)} custom-call(bf16[2,2,3,8,16,384]{5,4,3,2,1,0:T(8,128)(2,1)} %exchange.1.pieces), custom_call_target="tpu_custom_call" | custom-call | tf_op jit(solution)/shard_map/arrange/pallas_call | solution.py:352

commit v3 on v2

--- a/solution.py
+++ b/solution.py
@@ -11,7 +11,6 @@
 NX, NY, NZ = 4, 8, 8
 MESH = pl.DeviceIdType.MESH
 SEND_ORDER = (4, 3, 5, 2, 6, 1, 7)
-WAIT_ORDER = (1, 7, 2, 6, 3, 5, 4)
 CHUNKS = 3
 BF16, F32 = jnp.bfloat16, jnp.float32
 
@@ -24,10 +23,10 @@
 
 def kernel(
     scale,
-    hid, emb, head, lse, tok, tgt,
+    hid, emb, head, aux,
     out,
-    H, E, HB, LSE, TOK, TGT, LP, RS, XF, G, P1, R1, S2, R2, R3, T, P4,
-    loc_sem, out_sem, sib_s, sib_r, head_s, head_r, rs_s, rs_r, ag_s, ag_r,
+    H, E, HB, AUX, LP, RS, XF, G, P1, R1, S2, R2, R3, T,
+    loc_sem, sib_s, sib_r, head_s, head_r, rs_s, rs_r, ag_s, ag_r,
     p1_s, p1_r, p2_s, p2_r, p3_s, p3_r, p4_s, p4_r, fw_s, fw_r,
 ):
     x = lax.axis_index("vocab")
@@ -61,6 +60,20 @@
     source = tuple(lax.rem(p // 2 + NX - x, NX) for p in pos2)
     own2 = tuple(p == x for p in source)
 
+    barrier = pltpu.get_barrier_semaphore()
+    for h in range(2):
+        for s in range(8):
+            @pl.when(jnp.logical_not(own2[h] & (pos2[h] == s)))
+            def _():
+                pl.semaphore_signal(
+                    barrier, inc=1, device_id=second_dev(h, source[h], s), device_id_type=MESH
+                )
+    for t in SEND_ORDER:
+        for h in range(2):
+            pl.semaphore_signal(barrier, inc=1, device_id=ring_dev(h, ring[h](t)), device_id_type=MESH)
+    for t in SEND_ORDER:
+        pl.semaphore_signal(barrier, inc=1, device_id=group_dev(lax.rem(m + t, 8)), device_id_type=MESH)
+
     mine = pl.ds(pl.multiple_of(c * tokens, tokens), tokens)
     theirs = pl.ds(pl.multiple_of(o * tokens, tokens), tokens)
     my_cols = pl.ds(pl.multiple_of(c * cols, cols), cols)
@@ -70,26 +83,10 @@
         pltpu.make_async_copy(head.at[:, pl.ds(pl.multiple_of(m * cols, cols), cols)], HB.at[my_rows, :], loc_sem.at[0]),
         pltpu.make_async_copy(hid.at[:, my_cols], H.at[mine, :], loc_sem.at[1]),
         pltpu.make_async_copy(emb.at[:, my_cols], E.at[mine, :], loc_sem.at[2]),
-        pltpu.make_async_copy(tok, TOK.at[c], loc_sem.at[3]),
-        pltpu.make_async_copy(lse, LSE.at[c], loc_sem.at[4]),
-        pltpu.make_async_copy(tgt, TGT.at[c], loc_sem.at[5]),
+        pltpu.make_async_copy(aux, AUX.at[c], loc_sem.at[3]),
     ]
     for copy in locals_:
         copy.start()
-
-    barrier = pltpu.get_barrier_semaphore()
-    for t in range(1, 8):
-        pl.semaphore_signal(barrier, inc=1, device_id=group_dev(lax.rem(m + t, 8)), device_id_type=MESH)
-    for t in range(1, 8):
-        for h in range(2):
-            pl.semaphore_signal(barrier, inc=1, device_id=ring_dev(h, ring[h](t)), device_id_type=MESH)
-    for h in range(2):
-        for s in range(8):
-            @pl.when(jnp.logical_not(own2[h] & (pos2[h] == s)))
-            def _():
-                pl.semaphore_signal(
-                    barrier, inc=1, device_id=second_dev(h, source[h], s), device_id_type=MESH
-                )
 
     pl.semaphore_wait(barrier, 37 - own2[0].astype(jnp.int32) - own2[1].astype(jnp.int32))
 
@@ -99,9 +96,7 @@
         copy = remote(head.at[:, pcols], HB.at[my_rows, :], head_s, head_r, dev(px, y, z, c))
         copy.start()
     sib = [
-        remote(tok, TOK.at[c], sib_s.at[0], sib_r.at[0], sibling),
-        remote(lse, LSE.at[c], sib_s.at[3], sib_r.at[3], sibling),
-        remote(tgt, TGT.at[c], sib_s.at[4], sib_r.at[4], sibling),
+        remote(aux, AUX.at[c], sib_s.at[0], sib_r.at[0], sibling),
         remote(emb.at[:, their_cols], E.at[mine, :], sib_s.at[1], sib_r.at[1], sibling),
         remote(hid.at[:, their_cols], H.at[mine, :], sib_s.at[2], sib_r.at[2], sibling),
     ]
@@ -109,11 +104,9 @@
         copy.start()
 
     sib_in = [
-        remote(TOK.at[o], TOK.at[o], sib_s.at[0], sib_r.at[0], sibling),
+        remote(AUX.at[o], AUX.at[o], sib_s.at[0], sib_r.at[0], sibling),
         remote(E.at[theirs, :], E.at[theirs, :], sib_s.at[1], sib_r.at[1], sibling),
         remote(H.at[theirs, :], H.at[theirs, :], sib_s.at[2], sib_r.at[2], sibling),
-        remote(LSE.at[o], LSE.at[o], sib_s.at[3], sib_r.at[3], sibling),
-        remote(TGT.at[o], TGT.at[o], sib_s.at[4], sib_r.at[4], sibling),
     ]
     sib_in[0].wait_recv()
     sib_in[1].wait_recv()
@@ -122,18 +115,16 @@
     vocab = NX * rows
     order = lax.broadcasted_iota(jnp.int32, (vocab, tokens), 0)
     ordered = rows * ((order // 4) % 4) + 4 * (order // 16) + order % 4
+    ordered = ordered.astype(F32)
     picks = jnp.concatenate(
-        [jnp.where(TOK[k] == ordered, 1.0, 0.0).astype(BF16) for k in range(2)], axis=1
+        [jnp.where(AUX[k, 1:2, :] == ordered, 1.0, 0.0).astype(BF16) for k in range(2)], axis=1
     )
     step = half // 3
     for k in range(6):
         s = slice(k * step, (k + 1) * step)
         G[:, s] = jnp.dot(picks, E[:, s], preferred_element_type=F32)
 
-    for copy in sib_in[2:]:
-        copy.wait_recv()
-    locals_[4].wait()
-    locals_[5].wait()
+    sib_in[2].wait_recv()
     locals_[1].wait()
     locals_[0].wait()
     heads = remote(HB.at[:(NX - 1) * rows, :], HB.at[:(NX - 1) * rows, :], head_s, head_r, sibling)
@@ -154,7 +145,7 @@
     for t in SEND_ORDER:
         p = lax.rem(m + t, 8)
         remote(XF.at[my16, :], XF.at[my16, :], ag_s, ag_r, group_dev(p)).start()
-    natural = lax.broadcasted_iota(jnp.int32, (vocab, tokens), 0)
+    natural = lax.broadcasted_iota(jnp.int32, (vocab, tokens), 0).astype(F32)
     swap_r = lax.broadcasted_iota(jnp.int32, (vocab, vocab), 0)
     swap_c = lax.broadcasted_iota(jnp.int32, (vocab, vocab), 1)
     swap = jnp.where(rows * ((swap_r // 4) % 4) + 4 * (swap_r // 16) + swap_r % 4 == swap_c, 1.0, 0.0).astype(BF16)
@@ -162,8 +153,8 @@
     parts = []
     for k in range(2):
         ex = XF[:, k * tokens:(k + 1) * tokens]
-        denominator = jnp.exp(LSE[k]) + jnp.sum(ex, axis=0, keepdims=True)
-        coefficients = ex / denominator - jnp.where(TGT[k] == natural, 1.0, 0.0)
+        denominator = jnp.exp(AUX[k, 0:1, :]) + jnp.sum(ex, axis=0, keepdims=True)
+        coefficients = ex / denominator - jnp.where(AUX[k, 2:3, :] == natural, 1.0, 0.0)
         parts.append(coefficients.astype(BF16))
     coef = jnp.concatenate(parts, axis=1)
     coef = jnp.dot(swap, coef, preferred_element_type=F32).astype(BF16)
@@ -236,20 +227,16 @@
         remote(R3.at[h, k, :7], R3.at[h, k, :7], p3_s.at[h, k], p3_r.at[h, k], sibling).wait_recv()
         for i in range(8):
             T[h, k, 2 * i:2 * i + 2, :] = R3[h, k, i]
-        P4[h, k] = T[h, k].astype(BF16)
+        out[h, c, k, pos[h]] = T[h, k].astype(BF16)
         slot = out.at[h, c, k, pos[h]]
         for t in SEND_ORDER:
-            p = ring[h](t)
-            remote(P4.at[h, k], slot, p4_s.at[h, k], p4_r.at[h, k, t], ring_dev(h, p)).start()
-        remote(P4.at[h, k], slot, fw_s.at[h, k], fw_r.at[h, k], sibling).start()
-        pltpu.make_async_copy(P4.at[h, k], slot, out_sem.at[h, k]).start()
+            remote(slot, slot, p4_s.at[h, k], p4_r.at[h, k], ring_dev(h, ring[h](t))).start()
 
     def fifth(q):
         h, k = q
-        for t in WAIT_ORDER:
-            slot = out.at[h, c, k, ring[h](8 - t)]
-            remote(slot, slot, p4_s.at[h, k], p4_r.at[h, k, t], sibling).wait_recv()
-            remote(slot, slot, fw_s.at[h, k], fw_r.at[h, k], sibling).start()
+        seven = out.at[h, c, k, :7]
+        remote(seven, seven, p4_s.at[h, k], p4_r.at[h, k], sibling).wait_recv()
+        remote(out.at[h, c, k], out.at[h, c, k], fw_s.at[h, k], fw_r.at[h, k], sibling).start()
 
     for step in (first, second, third, fourth, fifth):
         for group in chunks:
@@ -262,27 +249,23 @@
     remote(RS.at[:7], RS.at[:7], rs_s, rs_r, sibling).wait_send()
     remote(XF.at[:7 * 16, :], XF.at[:7 * 16, :], ag_s, ag_r, sibling).wait_send()
     for h, k in [q for group in chunks for q in group]:
-        remote(P1.at[h, k, :7], P1.at[h, k, :7], p1_s.at[h, k], p1_r.at[h, k], sibling).wait_send()
+        seven = P1.at[h, k, :7]
+        remote(seven, seven, p1_s.at[h, k], p1_r.at[h, k], sibling).wait_send()
         remote(R3.at[h, k, :7], R3.at[h, k, :7], p3_s.at[h, k], p3_r.at[h, k], sibling).wait_send()
-        remote(P1.at[h, k, :7], P1.at[h, k, :7], p4_s.at[h, k], p4_r.at[h, k, 0], sibling).wait_send()
+        remote(P1.at[h, k, :7], P1.at[h, k, :7], p4_s.at[h, k], p4_r.at[h, k], sibling).wait_send()
         second_waits((h, k), lambda copy: copy.wait_send())
-        pltpu.make_async_copy(P4.at[h, k], out.at[h, c, k, pos[h]], out_sem.at[h, k]).wait()
         remote(out.at[h, o, k], out.at[h, o, k], fw_s.at[h, k], fw_r.at[h, k], sibling).wait()
 
 
-def arrange(pieces, result, held, made, in_sem, out_sem):
+def arrange(pieces, result, made, out_sem):
     width = pieces.shape[-1]
     half = CHUNKS * width
     me = lax.axis_index("vocab")
     places = [(h, c, k) for k in range(CHUNKS) for h in range(2) for c in range(2)]
-    loads = [pltpu.make_async_copy(pieces.at[q], held.at[q], in_sem.at[q]) for q in places]
-    for copy in loads:
-        copy.start()
     stores = []
-    for (h, c, k), load in zip(places, loads):
-        load.wait()
+    for h, c, k in places:
         for g in range(2):
-            group = [held[h, c, k, 4 * g + j].astype(F32) for j in range(4)]
+            group = [pieces[h, c, k, 4 * g + j].astype(F32) for j in range(4)]
             for x in range(NX):
                 block = jnp.concatenate([p[4 * x:4 * x + 4, :] for p in group], axis=0)
                 start = (2 * x + c) * 2 * half + h * half + k * width
@@ -304,20 +287,22 @@
     rows, model = head_block.shape
     cols, width_, vocab = width // 2, width // 4 // CHUNKS, rows * NX
     scale = math.sqrt(vocab / (tokens * lax.axis_size("dp")))
-    hbm = pl.BlockSpec(memory_space=pl.ANY)
+    line = lax.broadcasted_iota(jnp.int32, (3, tokens), 0)
+    ids = jnp.where(line == 1, token_ids[None, :], target_ids[None, :]).astype(F32)
+    aux = jnp.where(line == 0, lse_rest[None, :], ids)
+    hbm = pl.BlockSpec(memory_space=pltpu.HBM)
+    vmem = pl.BlockSpec(memory_space=pltpu.VMEM)
     dma = pltpu.SemaphoreType.DMA
     pieces = pl.pallas_call(
         functools.partial(kernel, scale),
         out_shape=jax.ShapeDtypeStruct((2, 2, CHUNKS, 8, 16, width_), BF16),
-        in_specs=[hbm] * 6,
-        out_specs=hbm,
+        in_specs=[hbm] * 4,
+        out_specs=vmem,
         scratch_shapes=[
             pltpu.VMEM((2 * tokens, cols), BF16),
             pltpu.VMEM((2 * tokens, cols), BF16),
             pltpu.VMEM((vocab, cols), BF16),
-            pltpu.VMEM((2, 1, tokens), F32),
-            pltpu.VMEM((2, 1, tokens), jnp.int32),
-            pltpu.VMEM((2, 1, tokens), jnp.int32),
+            pltpu.VMEM((2, 3, tokens), F32),
             pltpu.VMEM((vocab, 2 * tokens), F32),
             pltpu.VMEM((8, 16, 2 * tokens), F32),
             pltpu.VMEM((vocab, 2 * tokens), F32),
@@ -328,39 +313,35 @@
             pltpu.VMEM((2, CHUNKS, 8, 2, width_), F32),
             pltpu.VMEM((2, CHUNKS, 8, 2, width_), F32),
             pltpu.VMEM((2, CHUNKS, 16, width_), F32),
-            pltpu.VMEM((2, CHUNKS, 16, width_), BF16),
-            dma((6,)),
-            dma((2, CHUNKS)),
-            dma((5,)), dma((5,)),
+            dma((4,)),
+            dma((3,)), dma((3,)),
             dma, dma,
             dma, dma,
             dma, dma,
             dma((2, CHUNKS)), dma((2, CHUNKS)),
             dma((2, CHUNKS)), dma((2, CHUNKS)),
             dma((2, CHUNKS)), dma((2, CHUNKS)),
-            dma((2, CHUNKS)), dma((2, CHUNKS, 8)),
+            dma((2, CHUNKS)), dma((2, CHUNKS)),
             dma((2, CHUNKS)), dma((2, CHUNKS)),
         ],
         compiler_params=pltpu.CompilerParams(
-            collective_id=0, has_side_effects=True, vmem_limit_bytes=60 * 1024 * 1024
+            collective_id=0, has_side_effects=True, vmem_limit_bytes=52 * 1024 * 1024
         ),
         name="exchange",
     )(
         hidden, embed_cot, head_block,
-        lse_rest.reshape(1, tokens), token_ids.reshape(1, tokens), target_ids.reshape(1, tokens),
+        aux,
     )
     return pl.pallas_call(
         arrange,
         out_shape=jax.ShapeDtypeStruct((rows, model), BF16),
-        in_specs=[hbm],
+        in_specs=[vmem],
         out_specs=hbm,
         scratch_shapes=[
-            pltpu.VMEM((2, 2, CHUNKS, 8, 16, width_), BF16),
             pltpu.VMEM((rows, model), BF16),
-            dma((2, 2, CHUNKS)),
             dma((2, 2, CHUNKS, NX)),
         ],
-        compiler_params=pltpu.CompilerParams(vmem_limit_bytes=60 * 1024 * 1024),
+        compiler_params=pltpu.CompilerParams(vmem_limit_bytes=16 * 1024 * 1024),
         name="arrange",
     )(pieces)
 

time: 64.1 us -> 62.5 us (0.975)
  Pallas kernels: 63.9 us -> 61.6 us
  other arithmetic: 0 us -> 0.76 us
    pallas_call x1, Pallas kernels: 61.4 us -> 60.1 us  [local(): pl.pallas_call(functools.partial(kernel, scale), out_shape=jax.ShapeDtype...]
    pallas_call x1, Pallas kernels: 2.53 us -> 1.44 us  [local(): pl.pallas_call(arrange, out_shape=jax.ShapeDtypeStruct((rows, model), BF1...]
    select_n x0 -> x1, other arithmetic: none -> 0.76 us  [local(): aux = jnp.where(line == 0, lse_rest[None, :], ids)]
where the time goes in v3:
time: 62.5 us; the launch traced here: 62.4 us
  Pallas kernels  61.6 us (99%)
  other arithmetic  0.76 us (1%)
    pallas_call x1, Pallas kernels, local(): pl.pallas_call(functools.partial(kernel, scale), out_shape=jax.ShapeDtype...  60.1 us
    pallas_call x1, Pallas kernels, local(): pl.pallas_call(arrange, out_shape=jax.ShapeDtypeStruct((rows, model), BF1...  1.44 us

profile of v3, /device:TPU:1, one launch (start us, length us, event | category | flops | bytes accessed | tf_op | source)
XLA Modules:
  0.0 62.4 jit_solution(11293291343173617904)
XLA Ops:
  0.0 0.8 %convert_select_fusion.aux = f32[3,128]{1,0:T(4,128)S(1)} fusion(s32[128]{0:T(128)} %param.11, s32[128]{0:T(128)} %param.10, f32[128]{0:T(128)} %param.9, pred[3]{0:T(512)(128)(4,1)S(1)} %get-tuple-element.5, pred[3]{0:T(512)(128)(4,1)S(1)} %get-tuple-element.6), kind=kLoop, calls=%fused_computation | loop fusion | flops 1152 | bytes 3078 | tf_op jit(solution)/shard_map/jit(_where)/select_n | solution.py:292
  0.8 60.1 %exchange.1.pieces = bf16[2,2,3,8,16,384]{5,4,3,2,1,0:T(8,128)(2,1)S(1)} custom-call(bf16[128,4608]{1,0:T(8,128)(2,1)} %hid.1, bf16[128,4608]{1,0:T(8,128)(2,1)} %emb.1, bf16[32,18432]{1,0:T(8,128)(2,1)} %head.1, f32[3,128]{1,0:T(4,128)S(1)} %convert_select_fusion.aux), custom_call_target="tpu_custom_call" | custom-call | tf_op jit(solution)/shard_map/exchange/pallas_call | solution.py:296
  60.9 1.4 %arrange.1 = bf16[32,18432]{1,0:T(8,128)(2,1)} custom-call(bf16[2,2,3,8,16,384]{5,4,3,2,1,0:T(8,128)(2,1)S(1)} %exchange.1.pieces), custom_call_target="tpu_custom_call" | custom-call | tf_op jit(solution)/shard_map/arrange/pallas_call | solution.py:335
  (1 shorter events, 0.0 us)

commit v4 on v3

--- a/solution.py
+++ b/solution.py
@@ -90,17 +90,17 @@
 
     pl.semaphore_wait(barrier, 37 - own2[0].astype(jnp.int32) - own2[1].astype(jnp.int32))
 
-    for t in (2, 1, 3):
-        px = lax.rem(x + t, NX)
-        pcols = pl.ds(pl.multiple_of((2 * px + c) * cols, cols), cols)
-        copy = remote(head.at[:, pcols], HB.at[my_rows, :], head_s, head_r, dev(px, y, z, c))
-        copy.start()
     sib = [
         remote(aux, AUX.at[c], sib_s.at[0], sib_r.at[0], sibling),
         remote(emb.at[:, their_cols], E.at[mine, :], sib_s.at[1], sib_r.at[1], sibling),
         remote(hid.at[:, their_cols], H.at[mine, :], sib_s.at[2], sib_r.at[2], sibling),
     ]
     for copy in sib:
+        copy.start()
+    for t in (2, 1, 3):
+        px = lax.rem(x + t, NX)
+        pcols = pl.ds(pl.multiple_of((2 * px + c) * cols, cols), cols)
+        copy = remote(head.at[:, pcols], HB.at[my_rows, :], head_s, head_r, dev(px, y, z, c))
         copy.start()
 
     sib_in = [
@@ -287,9 +287,8 @@
     rows, model = head_block.shape
     cols, width_, vocab = width // 2, width // 4 // CHUNKS, rows * NX
     scale = math.sqrt(vocab / (tokens * lax.axis_size("dp")))
-    line = lax.broadcasted_iota(jnp.int32, (3, tokens), 0)
-    ids = jnp.where(line == 1, token_ids[None, :], target_ids[None, :]).astype(F32)
-    aux = jnp.where(line == 0, lse_rest[None, :], ids)
+    ids = jnp.pad(token_ids[None], ((1, 1), (0, 0))) + jnp.pad(target_ids[None], ((2, 0), (0, 0)))
+    aux = jnp.pad(lse_rest[None], ((0, 2), (0, 0))) + ids.astype(F32)
     hbm = pl.BlockSpec(memory_space=pltpu.HBM)
     vmem = pl.BlockSpec(memory_space=pltpu.VMEM)
     dma = pltpu.SemaphoreType.DMA

time: 62.5 us -> 62.4 us (level)
    select_n x1 -> x0, other arithmetic: 0.76 us -> none  [local(): aux = jnp.where(line == 0, lse_rest[None, :], ids)]
    add x0 -> x1, other arithmetic: none -> 0.7 us  [local(): aux = jnp.pad(lse_rest[None], ((0, 2), (0, 0))) + ids.astype(F32)]
where the time goes in v4:
time: 62.4 us; the launch traced here: 62.3 us
  Pallas kernels  61.6 us (99%)
  other arithmetic  0.7 us (1%)
    pallas_call x1, Pallas kernels, local(): pl.pallas_call(functools.partial(kernel, scale), out_shape=jax.ShapeDtype...  60.1 us
    pallas_call x1, Pallas kernels, local(): pl.pallas_call(arrange, out_shape=jax.ShapeDtypeStruct((rows, model), BF1...  1.44 us

profile of v4, /device:TPU:1, one launch (start us, length us, event | category | flops | bytes accessed | tf_op | source)
XLA Modules:
  0.0 62.3 jit_solution(14394922803024494539)
XLA Ops:
  0.0 0.7 %convert_add_fusion.aux = f32[3,128]{1,0:T(4,128)S(1)} fusion(s32[1,128]{1,0:T(1,128)} %bitcast.3, s32[1,128]{1,0:T(1,128)} %bitcast.4, f32[1,128]{1,0:T(1,128)} %bitcast.5), kind=kLoop, calls=%fused_computation | loop fusion | flops 1152 | bytes 3072 | tf_op jit(solution)/shard_map/add | solution.py:291
  0.7 60.1 %exchange.1.pieces = bf16[2,2,3,8,16,384]{5,4,3,2,1,0:T(8,128)(2,1)S(1)} custom-call(bf16[128,4608]{1,0:T(8,128)(2,1)} %hid.1, bf16[128,4608]{1,0:T(8,128)(2,1)} %emb.1, bf16[32,18432]{1,0:T(8,128)(2,1)} %head.1, f32[3,128]{1,0:T(4,128)S(1)} %convert_add_fusion.aux), custom_call_target="tpu_custom_call" | custom-call | tf_op jit(solution)/shard_map/exchange/pallas_call | solution.py:295
  60.9 1.4 %arrange.1 = bf16[32,18432]{1,0:T(8,128)(2,1)} custom-call(bf16[2,2,3,8,16,384]{5,4,3,2,1,0:T(8,128)(2,1)S(1)} %exchange.1.pieces), custom_call_target="tpu_custom_call" | custom-call | tf_op jit(solution)/shard_map/arrange/pallas_call | solution.py:334
